TPU v7x, 32 devices: a whole 2x2x4 slice. The times are simulated.
32 devices in a mesh: img: 4 (over y, x), ori: 8 (over z, core).
Axes of the slice: x: 2, y: 2, z: 4, core: 2. Of those that a mesh axis runs over, the one named last changes fastest.
Arguments:
- images: bfloat16 [1024, 2, 8192], P('img'), may hold values from -24 to 24
- projections: bfloat16 [1024, 2, 8192], P('ori'), may hold values from -0.2421875 to 0.2421875
- noise_weight: float32 [8192], replicated, may hold values from 0.25 to 4
- shift_ids: int32 [1024, 4], P('img'), may hold values from 0 to 48
- owner_ids: int32 [1024, 64], P('ori', 'img'), may hold values from 0 to 31, as said below
- cell_ids: int32 [1024, 64], P('ori', 'img'), may hold values from 0 to 4095
- weight_ids: int32 [1024, 64], P('ori', 'img'), may hold values from 0 to 63
- interp_table: bfloat16 [64, 128, 128], replicated, may hold values from -0.5 to 0.5
Outputs:
- realspace: float32 [2, 256, 256, 256], P(None, 'img', 'ori')
- loglik: float32 [1024], P('img')
Inputs may be any that keep to these rules, and one draw needn't show every extreme that they name: `owner_ids`: among the blocks of one device (rows of one index of ori, columns of one index of img), at most 192 name any one owner; one owner is named exactly 192 times by the blocks of every device.
All inputs are finite; a program needn't handle non-finite values.
Results may differ from a plain program's by a relative error of at most 0.0058.
Values may be sent and summed in bfloat16 or wider, within the bound.
A program may use at most 192 MiB of HBM per device.

v0:
```python
import functools
import math

import jax
import jax.numpy as jnp
import ml_dtypes
import numpy as np
from jax import lax
from jax.experimental import pallas as pl
from jax.experimental.pallas import tpu as pltpu
from jax.sharding import PartitionSpec as P

IMGBOX = 128
BOX = 256
GRID = 7
VMEM_BYTES = 56 * 1024 * 1024
F32 = jnp.float32
BF16 = jnp.bfloat16


def split_table(table, terms):
    rest = table.astype(np.float32)
    pieces = []
    for _ in range(terms):
        piece = rest.astype(ml_dtypes.bfloat16)
        pieces.append(piece)
        rest = rest - piece.astype(np.float32)
    return pieces


def phase_tables(coef_count):
    coef = np.arange(coef_count)
    kx, ky = coef % IMGBOX - IMGBOX // 2, coef // IMGBOX
    shift = np.arange(64)
    dx, dy = shift % GRID - GRID // 2, shift // GRID - GRID // 2
    turns = (kx[None, :] * dx[:, None] + ky[None, :] * dy[:, None]) % IMGBOX
    angles = turns * (-2.0 * math.pi / IMGBOX)
    return (
        np.concatenate(split_table(np.cos(angles), 3)),
        np.concatenate(split_table(np.sin(angles), 3)),
    )


def dft_tables():
    index = np.arange(BOX)
    angles = (index[:, None] * index[None, :] % BOX) * (2.0 * math.pi / BOX)
    factor = 1.0 / math.sqrt(BOX)
    return np.cos(angles) * factor, np.sin(angles) * factor


def z_tables(block_len, chunks):
    cosine, sine = dft_tables()
    span = BOX // chunks
    full = np.zeros((2, BOX, chunks, 2, span))
    cos_c, sin_c = cosine.reshape(BOX, chunks, span), sine.reshape(BOX, chunks, span)
    full[0, :, :, 0], full[0, :, :, 1] = cos_c, sin_c
    full[1, :, :, 0], full[1, :, :, 1] = -sin_c, cos_c
    full = full.reshape(2, BOX // block_len, block_len, 2 * BOX).transpose(1, 0, 2, 3)
    full = full.reshape(BOX // block_len, 2 * block_len, 2 * BOX)
    return np.stack(split_table(full, 2), axis=1)


def cos_sin_split():
    cosine, sine = dft_tables()
    return np.stack(split_table(cosine, 2) + split_table(sine, 2))


def turn_table(width):
    half = width // 2
    table = np.zeros((width, width), np.float32)
    for j in range(half):
        table[j, half + j] = 1.0
        table[half + j, j] = -1.0
    return table.astype(ml_dtypes.bfloat16)


def dot(left, right):
    return jnp.dot(left, right, preferred_element_type=F32)


def params():
    return pltpu.CompilerParams(vmem_limit_bytes=VMEM_BYTES)


def aligned_chunk(pick, cos_ref, sin_ref, img_ref):
    cosine = dot(pick, cos_ref[...])
    sine = dot(pick, sin_ref[...])
    real = img_ref[0].astype(F32)
    imag = img_ref[1].astype(F32)
    new_real = (real * cosine - imag * sine).astype(BF16)
    new_imag = (real * sine + imag * cosine).astype(BF16)
    return new_real, new_imag


def score_kernel(steps, pick_ref, cos_ref, sin_ref, img_ref, proj_ref, noise_ref, out_ref, norm):
    step = pl.program_id(0)
    rows = img_ref.shape[1]
    chunk = img_ref.shape[2]

    @pl.when(step == 0)
    def _():
        out_ref[...] = jnp.zeros_like(out_ref)
        norm[...] = jnp.zeros_like(norm)

    noise = noise_ref[...]
    weighted = []
    for part in range(2):
        proj = proj_ref[part].astype(F32)
        scaled = proj * noise
        weighted.append(scaled.astype(BF16))
        power = scaled * proj
        for lane in range(0, chunk, 128):
            norm[...] += power[:, lane : lane + 128]
    dims = (((1,), (1,)), ((), ()))
    for group in range(pick_ref.shape[0] // rows):
        span = pl.ds(group * rows, rows)
        real, imag = aligned_chunk(pick_ref[span, :], cos_ref, sin_ref, img_ref)
        out_ref[span, :] += lax.dot_general(
            real, weighted[0], dims, preferred_element_type=F32
        ) + lax.dot_general(imag, weighted[1], dims, preferred_element_type=F32)

    @pl.when(step == steps - 1)
    def _():
        out_ref[...] -= 0.5 * jnp.sum(norm[...].T, axis=0, keepdims=True)


def slice_kernel(pick_ref, cos_ref, sin_ref, img_ref, prob_ref, out_ref):
    rows = img_ref.shape[1]
    block_len = out_ref.shape[3]
    totals = [0.0, 0.0]
    for group in range(pick_ref.shape[0] // rows):
        span = pl.ds(group * rows, rows)
        pair = aligned_chunk(pick_ref[span, :], cos_ref, sin_ref, img_ref)
        prob = prob_ref[:, span]
        totals = [total + dot(prob, value) for total, value in zip(totals, pair)]
    for part in range(2):
        for block in range(out_ref.shape[0]):
            piece = totals[part][:, block * block_len : (block + 1) * block_len]
            out_ref[block, part] = piece.astype(BF16)


def place_kernel(tables, group, value_ref, id_ref, table_ref, slot_ref, out_ref, terms):
    step = pl.program_id(0)
    blocks, _, orient, block_len = value_ref.shape
    batch = 8

    @pl.when(step == 0)
    def _():
        @pl.loop(0, blocks // group)
        def _(index):
            span = pl.ds(index * group, group)
            values = value_ref[span].reshape(group * 2 * orient, block_len)
            ids = id_ref[span].reshape(group * 2 * orient, block_len)
            total = jnp.zeros(values.shape, F32)
            for first in range(0, tables, batch):
                picked = [
                    jnp.where(ids == jnp.asarray(w, BF16), values, jnp.zeros_like(values))
                    for w in range(first, first + batch)
                ]
                total += dot(
                    jnp.concatenate(picked, axis=1),
                    table_ref[first * block_len : (first + batch) * block_len, :],
                )
            total = total.astype(BF16).reshape(group, 2, orient, block_len)
            for block in range(group):
                place = pl.multiple_of((index * group + block) * orient, orient)
                for part in range(2):
                    lanes = slice(part * block_len, (part + 1) * block_len)
                    terms[pl.ds(place, orient), lanes] = total[block, part]

    rows = out_ref.shape[0]
    wanted = lax.broadcasted_iota(jnp.int32, (rows, terms.shape[0]), 0) + step * rows
    hit = jnp.where(wanted == slot_ref[...], 1.0, 0.0).astype(BF16)
    out_ref[...] = dot(hit, terms[...]).astype(BF16)


def volume_kernel(depth, cell_ref, term_ref, dft_ref, out_ref):
    step = pl.program_id(0)
    chunks, rows, width = out_ref.shape
    z_blocks = dft_ref.shape[0]
    first = (lax.broadcasted_iota(jnp.int32, (rows, depth), 0) + step * rows) * z_blocks
    result = jnp.zeros((rows, chunks * width), F32)
    for half in range(z_blocks):
        total = jnp.zeros((rows, term_ref.shape[1]), F32)
        for start in range(0, term_ref.shape[0], depth):
            hit = jnp.where(first + half == cell_ref[:, start : start + depth], 1.0, 0.0)
            total += dot(hit.astype(BF16), term_ref[start : start + depth, :])
        total = total.astype(BF16)
        result += dot(total, dft_ref[half, 0]) + dot(total, dft_ref[half, 1])
    for chunk in range(chunks):
        out_ref[chunk] = result[:, chunk * width : (chunk + 1) * width].astype(BF16)


def y_kernel(dft_ref, turn_ref, in_ref, out_ref):
    sources, tall, width = in_ref.shape
    targets, count, span, _ = out_ref.shape
    y_span = tall // count
    plain, turned = [], []
    for x in range(count):
        column = jnp.concatenate(
            [in_ref[source, x * y_span : (x + 1) * y_span, :] for source in range(sources)], axis=0
        )
        plain.append(column)
        turned.append(dot(column, turn_ref[...]).astype(BF16))
    plain = jnp.concatenate(plain, axis=1)
    turned = jnp.concatenate(turned, axis=1)
    result = dot(dft_ref[0], plain) + dot(dft_ref[1], plain)
    result += dot(dft_ref[2], turned) + dot(dft_ref[3], turned)
    for x in range(count):
        for target in range(targets):
            out_ref[target, x] = result[
                target * span : (target + 1) * span, x * width : (x + 1) * width
            ].astype(BF16)


def x_kernel(dft_ref, in_ref, out_ref, wide, left):
    box, count, width = in_ref.shape
    half = width // 2
    wide[...] = in_ref[...].astype(F32)
    for y in range(count):
        row = wide[:, y, :].T
        left[0, y * width : (y + 1) * width, :] = row.astype(BF16)
        left[1, y * width : (y + 1) * width, :] = jnp.concatenate(
            [-row[half:], row[:half]], axis=0
        ).astype(BF16)
    result = dot(left[0], dft_ref[0]) + dot(left[0], dft_ref[1])
    result += dot(left[1], dft_ref[2]) + dot(left[1], dft_ref[3])
    for y in range(count):
        out_ref[:, y, :] = result[y * width : (y + 1) * width, :]


def whole(shape):
    return pl.BlockSpec(shape, lambda i: (0,) * len(shape))


def combine(pairs):
    peaks, totals = pairs[:, 0], pairs[:, 1]
    peak = jnp.max(peaks, axis=0)
    return peak, jnp.sum(totals * jnp.exp(peaks - peak), axis=0)


def local(
    images, projections, noise_weight, shift_ids, owner_ids, cell_ids, weight_ids, interp_table
):
    n_img, n_ori = lax.axis_size("img"), lax.axis_size("ori")
    devices = n_img * n_ori
    row_count, _, coef_count = images.shape
    shift_count = shift_ids.shape[1]
    orient = projections.shape[0]
    tables, block_len, _ = interp_table.shape
    rows = row_count * shift_count
    blocks = owner_ids.shape[1]
    block_count = orient * blocks
    capacity = max(2, (3 * block_count + devices - 1) // devices)
    slots = devices * capacity

    owners = owner_ids.T.reshape(-1)
    cells = cell_ids.T.reshape(-1)
    group = math.gcd(block_count, 128)
    named = owners[:, None] == jnp.arange(devices, dtype=jnp.int32)[None, :]
    named_b = named.astype(BF16).reshape(-1, group, devices)
    lower = jnp.tril(jnp.ones((group, group), BF16))
    within = jnp.einsum("ij,gjd->gid", lower, named_b, preferred_element_type=F32)
    before = jnp.cumsum(within[:, -1], axis=0) - within[:, -1]
    running = (within + before[:, None, :]).reshape(block_count, devices)
    rank = jnp.sum(jnp.where(named, running, 0.0), axis=1).astype(jnp.int32) - 1
    slot_ids = owners * capacity + rank
    send_cells = (
        jnp.full((slots,), -1, jnp.int32).at[slot_ids].set(cells).reshape(devices, capacity)
    )
    got_cells = lax.all_to_all(
        send_cells, ("img", "ori"), split_axis=0, concat_axis=0, tiled=True
    ).reshape(1, slots)
    ids = jnp.broadcast_to(
        weight_ids.T.astype(BF16)[:, None, :, None], (blocks, 2, orient, block_len)
    )

    chunk = math.gcd(coef_count, 1024)
    steps = coef_count // chunk
    cos_table, sin_table = phase_tables(coef_count)
    depth = cos_table.shape[0]
    pick = (
        shift_ids.T.reshape(-1)[:, None] == jnp.arange(depth, dtype=jnp.int32)[None, :] % 64
    ).astype(BF16)
    image_parts = images.transpose(1, 0, 2)
    proj_parts = projections.transpose(1, 0, 2)
    table_spec = pl.BlockSpec((depth, chunk), lambda i: (0, i))
    image_spec = pl.BlockSpec((2, row_count, chunk), lambda i: (0, 0, i))
    scores = pl.pallas_call(
        functools.partial(score_kernel, steps),
        grid=(steps,),
        out_shape=jax.ShapeDtypeStruct((rows, orient), F32),
        in_specs=[
            whole((rows, depth)),
            table_spec,
            table_spec,
            image_spec,
            pl.BlockSpec((2, orient, chunk), lambda i: (0, 0, i)),
            pl.BlockSpec((1, chunk), lambda i: (0, i)),
        ],
        out_specs=whole((rows, orient)),
        scratch_shapes=[pltpu.VMEM((orient, 128), F32)],
        compiler_params=params(),
        name="scores",
    )(pick, cos_table, sin_table, image_parts, proj_parts, noise_weight.reshape(1, -1))
    scores = scores.reshape(shift_count, row_count, orient)
    local_peak = jnp.max(scores, axis=(0, 2))
    local_total = jnp.sum(jnp.exp(scores - local_peak[None, :, None]), axis=(0, 2))
    peak, total = combine(lax.all_gather(jnp.stack([local_peak, local_total]), "ori"))
    loglik = peak + jnp.log(total)
    prob = (jnp.exp(scores - peak[None, :, None]) / total[None, :, None]).astype(BF16)
    prob = prob.reshape(rows, orient).T

    per_step = chunk // block_len
    partial_sums = pl.pallas_call(
        slice_kernel,
        grid=(steps,),
        out_shape=jax.ShapeDtypeStruct((coef_count // block_len, 2, orient, block_len), BF16),
        in_specs=[
            whole((rows, depth)),
            table_spec,
            table_spec,
            image_spec,
            whole((orient, rows)),
        ],
        out_specs=pl.BlockSpec((per_step, 2, orient, block_len), lambda i: (i, 0, 0, 0)),
        compiler_params=params(),
        name="slices",
    )(pick, cos_table, sin_table, image_parts, prob)
    slices = lax.psum_scatter(partial_sums, "img", scatter_dimension=0, tiled=True)

    tile = math.gcd(slots, 512)
    value_shape = (blocks, 2, orient, block_len)
    send_terms = pl.pallas_call(
        functools.partial(place_kernel, tables, math.gcd(blocks, 4)),
        grid=(slots // tile,),
        out_shape=jax.ShapeDtypeStruct((slots, 2 * block_len), BF16),
        in_specs=[
            whole(value_shape),
            whole(value_shape),
            whole((tables * block_len, block_len)),
            whole((1, block_count)),
        ],
        out_specs=pl.BlockSpec((tile, 2 * block_len), lambda i: (i, 0)),
        scratch_shapes=[pltpu.VMEM((block_count, 2 * block_len), BF16)],
        compiler_params=params(),
        name="place",
    )(
        slices,
        ids,
        interp_table.reshape(tables * block_len, block_len),
        slot_ids.reshape(1, block_count),
    )
    got_terms = lax.all_to_all(
        send_terms.reshape(devices, capacity, 2 * block_len),
        ("img", "ori"),
        split_axis=0,
        concat_axis=0,
        tiled=True,
    ).reshape(slots, 2 * block_len)

    x_span, y_span = BOX // n_ori, BOX // n_img
    pencils = x_span * y_span
    width = 2 * (BOX // n_img)
    z_table = z_tables(block_len, n_img)
    tile = math.gcd(pencils, 256)
    pencil_parts = pl.pallas_call(
        functools.partial(volume_kernel, math.gcd(slots, 2048)),
        grid=(pencils // tile,),
        out_shape=jax.ShapeDtypeStruct((n_img, pencils, width), BF16),
        in_specs=[whole((1, slots)), whole((slots, 2 * block_len)), whole(z_table.shape)],
        out_specs=pl.BlockSpec((n_img, tile, width), lambda i: (0, i, 0)),
        compiler_params=params(),
        name="volume",
    )(got_cells, got_terms, z_table)
    pencil_parts = lax.all_to_all(pencil_parts, "img", split_axis=0, concat_axis=0, tiled=True)

    dft = cos_sin_split()
    count = math.gcd(x_span, 4)
    pencil_parts = pl.pallas_call(
        y_kernel,
        grid=(x_span // count,),
        out_shape=jax.ShapeDtypeStruct((n_ori, x_span, BOX // n_ori, width), BF16),
        in_specs=[
            whole(dft.shape),
            whole((width, width)),
            pl.BlockSpec((n_img, count * y_span, width), lambda i: (0, i, 0)),
        ],
        out_specs=pl.BlockSpec((n_ori, count, BOX // n_ori, width), lambda i: (0, i, 0, 0)),
        compiler_params=params(),
        name="along_y",
    )(dft, turn_table(width), pencil_parts)
    pencil_parts = lax.all_to_all(pencil_parts, "ori", split_axis=0, concat_axis=0, tiled=True)

    y_out = BOX // n_ori
    count = math.gcd(y_out, 16)
    realspace = pl.pallas_call(
        x_kernel,
        grid=(y_out // count,),
        out_shape=jax.ShapeDtypeStruct((width, y_out, BOX), F32),
        in_specs=[
            whole(dft.shape),
            pl.BlockSpec((BOX, count, width), lambda i: (0, i, 0)),
        ],
        out_specs=pl.BlockSpec((width, count, BOX), lambda i: (0, i, 0)),
        scratch_shapes=[
            pltpu.VMEM((BOX, count, width), F32),
            pltpu.VMEM((2, count * width, BOX), BF16),
        ],
        compiler_params=params(),
        name="along_x",
    )(dft, pencil_parts.reshape(BOX, y_out, width))
    return realspace.reshape(2, width // 2, y_out, BOX), loglik


def solution(mesh):
    placed = (
        P("img", None, None),
        P("ori", None, None),
        P(),
        P("img", None),
        P("ori", "img"),
        P("ori", "img"),
        P("ori", "img"),
        P(),
    )
    return jax.shard_map(
        local,
        mesh=mesh,
        in_specs=placed,
        out_specs=(P(None, "img", "ori", None), P("img")),
        check_vma=False,
    )
```

profile of v0, /device:TPU:0, one launch (start us, length us, event | category | flops | bytes accessed | tf_op | source)
XLA Modules:
  0.0 392.5 jit_solution(2802752988811106285)
XLA Ops:
  7.2 0.0 reduce-scatter.2.cloned.1.call-start
  7.2 0.0 copy-start.6
  7.2 0.0 copy-start.2
  7.2 12.7 %copy.53 = bf16[256,2,8192]{2,0,1:T(8,128)(2,1)} copy(bf16[256,2,8192]{2,1,0:T(2,128)(2,1)} %param.13) | data formatting | bytes 16777216 | tf_op args[0]
  19.9 0.0 copy-done.6
  19.9 0.0 copy-done.2
  19.9 4.6 %copy.54 = bf16[128,2,8192]{2,0,1:T(8,128)(2,1)} copy(bf16[128,2,8192]{2,1,0:T(2,128)(2,1)S(1)} %copy-done.2) | data formatting | bytes 8388608 | tf_op args[1]
  24.6 1.0 compare_convert_fusion.pick_ref
  25.6 30.9 %scores.1 = f32[1024,128]{1,0:T(8,128)} custom-call(bf16[1024,192]{1,0:T(8,128)(2,1)} %compare_convert_fusion.pick_ref, bf16[192,8192]{1,0:T(8,128)(2,1)} %constant.47.clone.cos_ref, bf16[192,8192]{1,0:T(8,128)(2,1)} %constant.48.clone.sin_ref, bf16[2,256,8192]{2,1,0:T(8,128)(2,1)} %bitcast.58, bf16[2,128,8192]{2,1,0:T(8,128)(2,1)} %bitcast.60, ...), custom_call_target="tpu_custom_call" | custom-call | tf_op jit(solution)/shard_map/scores/pallas_call | solution.py:289
  56.5 1.2 copy.37
  57.8 1.2 reduce_max.21
  59.1 1.4 exponential_reduce_fusion
  60.5 14.4 %all-gather.1 = f32[8,2,256]{2,1,0:T(2,128)S(1)} all-gather(f32[1,2,256]{2,1,0:T(2,128)S(1)} %maximum_bitcast_fusion), channel_id=2, replica_groups=mesh['img'=4,'ori'=8] {'ori'}, dimensions={0}, use_global_device_ids=true | all-gather | bytes 18432 | tf_op jit(solution)/shard_map/all_gather | solution.py:309
  75.0 0.8 fusion.prob_ref
  75.8 26.4 %slices.1 = bf16[64,2,128,128]{3,2,1,0:T(8,128)(2,1)} custom-call(bf16[1024,192]{1,0:T(8,128)(2,1)} %compare_convert_fusion.pick_ref, bf16[192,8192]{1,0:T(8,128)(2,1)} %constant.47.clone.cos_ref, bf16[192,8192]{1,0:T(8,128)(2,1)} %constant.48.clone.sin_ref, bf16[2,256,8192]{2,1,0:T(8,128)(2,1)} %bitcast.59, bf16[128,1024]{1,0:T(8,128)(2,1)} %fusion.prob_ref), custom_call_target="tpu_custom_call" | custom-call | tf_op jit(solution)/shard_map/slices/pallas_call | solution.py:315
  102.2 0.0 copy-start.3
  102.2 0.0 copy-start.5
  102.2 0.0 reduce-scatter.2.cloned.1.call-update
  102.2 0.7 copy-done.3
  102.9 0.2 convolution_bitcast_fusion
  103.1 0.1 slice.13
  103.2 0.2 copy.33
  103.4 0.2 copy.34
  103.6 0.3 subtract_reduce_fusion
  103.9 0.1 select_reduce_fusion
  104.0 0.0 copy-start.4
  104.1 8.2 %scatter_custom_fusion = s32[6144]{0:T(1024)S(1)} fusion(s32[2048]{0:T(1024)S(1)} %bitcast.76, s32[2048]{0:T(1024)} %bitcast.79, s32[]{:T(128)} %constant.20.clone.1), kind=kCustom, calls=%fused_computation.18 | custom fusion | bytes 25088 | tf_op jit(solution)/shard_map/scatter | solution.py:269
  112.3 0.7 all_to_all.15
  113.0 4.6 %all-to-all-start = ((s32[32,1,192]{2,1,0:T(1,128)}), s32[32,1,192]{2,1,0:T(1,128)S(1)}, u32[]{:S(2)}, u32[]{:S(2)}) async-start(s32[32,1,192]{2,1,0:T(1,128)} %all_to_all.15), calls=%async_computation | async-start | bytes 65536 | tf_op jit(solution)/shard_map/all_to_all | solution.py:271
  117.6 0.0 copy-done.5
  117.7 37.6 %reduce-scatter.2.cloned.1.call-done.value_ref = bf16[16,2,128,128]{3,2,1,0:T(8,128)(2,1)} async-done(((bf16[64,2,128,128]{3,2,1,0:T(8,128)(2,1)}), bf16[16,2,128,128]{3,2,1,0:T(8,128)(2,1)}) %reduce-scatter.2.cloned.1.call-update) | async-done | bytes 1048592 | tf_op jit(solution)/shard_map/reduce_scatter | solution.py:330
  155.2 1.4 broadcast_in_dim.32.id_ref
  156.7 0.0 copy-done.4
  156.7 29.7 %place.1 = bf16[6144,256]{1,0:T(8,128)(2,1)} custom-call(bf16[16,2,128,128]{3,2,1,0:T(8,128)(2,1)} %reduce-scatter.2.cloned.1.call-done.value_ref, bf16[16,2,128,128]{3,2,1,0:T(8,128)(2,1)} %broadcast_in_dim.32.id_ref, bf16[8192,128]{1,0:T(8,128)(2,1)} %bitcast.65, s32[1,2048]{1,0:T(1,128)} %bitcast.69), custom_call_target="tpu_custom_call" | custom-call | tf_op jit(solution)/shard_map/place/pallas_call | solution.py:334
  186.4 0.0 all-to-all-done
  186.4 4.6 %all-to-all-start.1 = ((bf16[32,192,256]{2,1,0:T(8,128)(2,1)}), bf16[32,192,256]{2,1,0:T(8,128)(2,1)S(1)}, u32[]{:S(2)}, u32[]{:S(2)}) async-start(bf16[32,192,256]{2,1,0:T(8,128)(2,1)} %bitcast.61), calls=%async_computation.2 | async-start | bytes 6291456 | tf_op jit(solution)/shard_map/all_to_all | solution.py:354
  191.0 0.1 reduce.7
  191.1 0.7 reshape.166.cell_ref
  191.7 71.8 %all-to-all-done.1 = bf16[32,192,256]{2,1,0:T(8,128)(2,1)S(1)} async-done(((bf16[32,192,256]{2,1,0:T(8,128)(2,1)}), bf16[32,192,256]{2,1,0:T(8,128)(2,1)S(1)}, u32[]{:S(2)}, u32[]{:S(2)}) %all-to-all-start.1) | async-done | bytes 3145760 | tf_op jit(solution)/shard_map/all_to_all | solution.py:354
  263.6 1.7 copy-done
  265.3 20.2 %volume.1 = bf16[4,2048,128]{2,1,0:T(8,128)(2,1)} custom-call(s32[1,6144]{1,0:T(1,128)} %reshape.166.cell_ref, bf16[6144,256]{1,0:T(8,128)(2,1)} %bitcast.62, bf16[2,2,256,512]{3,2,1,0:T(8,128)(2,1)} %constant.49.clone.dft_ref), custom_call_target="tpu_custom_call" | custom-call | tf_op jit(solution)/shard_map/volume/pallas_call | solution.py:367
  285.5 29.9 %all_to_all.24.in_ref = bf16[4,2048,128]{2,1,0:T(8,128)(2,1)} all-to-all(bf16[4,2048,128]{2,1,0:T(8,128)(2,1)} %volume.1), channel_id=1, replica_groups=mesh['img'=4,'ori'=8] {'img'}, dimensions={0} | all-to-all | bytes 4194304 | tf_op jit(solution)/shard_map/all_to_all | solution.py:376
  315.4 7.6 %along_y.1 = bf16[8,32,32,128]{3,2,1,0:T(8,128)(2,1)} custom-call(bf16[4,256,256]{2,1,0:T(8,128)(2,1)} %constant.50.clone.dft_ref, bf16[128,128]{1,0:T(8,128)(2,1)} %constant.51.clone.turn_ref, bf16[4,2048,128]{2,1,0:T(8,128)(2,1)} %all_to_all.24.in_ref), custom_call_target="tpu_custom_call" | custom-call | tf_op jit(solution)/shard_map/along_y/pallas_call | solution.py:380
  323.0 3.6 all-to-all-start.3
  326.6 0.6 log_add_fusion
  327.2 48.4 %all-to-all-done.3 = bf16[8,32,32,128]{3,2,1,0:T(8,128)(2,1)S(1)} async-done(((bf16[8,32,32,128]{3,2,1,0:T(8,128)(2,1)}), bf16[8,32,32,128]{3,2,1,0:T(8,128)(2,1)S(1)}, u32[]{:S(2)}, u32[]{:S(2)}) %all-to-all-start.3) | async-done | bytes 2097184 | tf_op jit(solution)/shard_map/all_to_all | solution.py:393
  375.6 1.3 copy-done.1
  377.0 8.7 %along_x.1 = f32[128,32,256]{2,1,0:T(8,128)} custom-call(bf16[4,256,256]{2,1,0:T(8,128)(2,1)} %constant.50.clone.dft_ref, bf16[256,32,128]{2,1,0:T(8,128)(2,1)} %bitcast.63), custom_call_target="tpu_custom_call" | custom-call | tf_op jit(solution)/shard_map/along_x/pallas_call | solution.py:397
  (21 shorter events, 0.2 us)
Async XLA Ops:
  7.2 148.1 %reduce-scatter.2.cloned.1.call-start = ((), (), s32[]{:S(2)}) async-start(), calls=%async_computation.5 | async-start | bytes 5242880 | tf_op jit(solution)/shard_map/reduce_scatter | solution.py:330
  7.2 12.7 %copy-start.6 = (s32[256,4]{0,1:T(4,128)S(1)}, s32[256,4]{0,1:T(4,128)}, u32[]{:S(2)}) copy-start(s32[256,4]{0,1:T(4,128)} %param.16) | copy-start | bytes 12292
  7.2 12.7 %copy-start.2 = (bf16[128,2,8192]{2,1,0:T(2,128)(2,1)S(1)}, bf16[128,2,8192]{2,1,0:T(2,128)(2,1)}, u32[]{:S(2)}) copy-start(bf16[128,2,8192]{2,1,0:T(2,128)(2,1)} %param.14) | copy-start | bytes 12582916
  102.2 0.7 copy-start.3
  102.2 15.4 %copy-start.5 = (s32[128,16]{0,1:T(8,128)S(1)}, s32[128,16]{0,1:T(8,128)}, u32[]{:S(2)}) copy-start(s32[128,16]{0,1:T(8,128)} %param.19) | copy-start | bytes 24580
  104.0 52.6 %copy-start.4 = (s32[16,128]{1,0:T(8,128)}, s32[16,128]{1,0:T(8,128)S(1)}, u32[]{:S(2)}) copy-start(s32[16,128]{1,0:T(8,128)S(1)} %add_add_fusion) | copy-start | bytes 24580
  113.0 73.3 %all-to-all-start = ((s32[32,1,192]{2,1,0:T(1,128)}), s32[32,1,192]{2,1,0:T(1,128)S(1)}, u32[]{:S(2)}, u32[]{:S(2)}) async-start(s32[32,1,192]{2,1,0:T(1,128)} %all_to_all.15), calls=%async_computation | async-start | bytes 65536 | tf_op jit(solution)/shard_map/all_to_all | solution.py:271
  186.4 77.2 %all-to-all-start.1 = ((bf16[32,192,256]{2,1,0:T(8,128)(2,1)}), bf16[32,192,256]{2,1,0:T(8,128)(2,1)S(1)}, u32[]{:S(2)}, u32[]{:S(2)}) async-start(bf16[32,192,256]{2,1,0:T(8,128)(2,1)} %bitcast.61), calls=%async_computation.2 | async-start | bytes 6291456 | tf_op jit(solution)/shard_map/all_to_all | solution.py:354
  263.6 1.7 copy-start
  323.0 52.6 %all-to-all-start.3 = ((bf16[8,32,32,128]{3,2,1,0:T(8,128)(2,1)}), bf16[8,32,32,128]{3,2,1,0:T(8,128)(2,1)S(1)}, u32[]{:S(2)}, u32[]{:S(2)}) async-start(bf16[8,32,32,128]{3,2,1,0:T(8,128)(2,1)} %along_y.1), calls=%async_computation.4 | async-start | bytes 4194304 | tf_op jit(solution)/shard_map/all_to_all | solution.py:393
  375.6 1.4 copy-start.1
Sparse Core Ops, SparseCore 0:
  102.4 52.8 reduce-scatter.1
where the time goes:
time: 393 us; the launch traced here: 392 us
  waiting for transfers between devices  158 us (40%)
  Pallas kernels  124 us (32%)
  blocking collectives  44.3 us (11%)
  local copies, waits for them, and re-layouts  33.8 us (9%)
  between operations  14.2 us (4%)
  starting transfers between devices  12.9 us (3%)
  other arithmetic  5.73 us (1%)
    all_to_all x1, waiting for transfers between devices, local(): lax.all_to_all(send_terms.reshape(devices, capacity, 2 * block_len), ('im...  71.8 us
    all_to_all x1, waiting for transfers between devices, local(): lax.all_to_all(pencil_parts, 'ori', split_axis=0, concat_axis=0, tiled=True)  48.4 us
    reduce_scatter x1, waiting for transfers between devices, local(): lax.psum_scatter(partial_sums, 'img', scatter_dimension=0, tiled=True)  37.6 us
    pallas_call x1, Pallas kernels, local(): pl.pallas_call(functools.partial(score_kernel, steps), grid=(steps,), out...  30.9 us
    all_to_all x1, blocking collectives, local(): lax.all_to_all(pencil_parts, 'img', split_axis=0, concat_axis=0, tiled=True)  29.9 us
    pallas_call x1, Pallas kernels, local(): pl.pallas_call(functools.partial(place_kernel, tables, math.gcd(blocks, 4...  29.7 us
    pallas_call x1, Pallas kernels, local(): pl.pallas_call(slice_kernel, grid=(steps,), out_shape=jax.ShapeDtypeStruc...  26.4 us
    unnamed x23, local copies, waits for them, and re-layouts  21 us
  transfers between devices with their start and end apart: 4, of which 3 were waited for; matrix products, arithmetic and copies ran while one was open for 3% of the time, Pallas kernels for 8%

commit v1 on v0

v1 whole, which is shorter than its diff:
```python
import functools
import math

import jax
import jax.numpy as jnp
import ml_dtypes
import numpy as np
from jax import lax
from jax.experimental import pallas as pl
from jax.experimental.pallas import tpu as pltpu
from jax.sharding import PartitionSpec as P

IMGBOX = 128
BOX = 256
GRID = 7
VMEM_BYTES = 56 * 1024 * 1024
F32 = jnp.float32
BF16 = jnp.bfloat16
MESH = pl.DeviceIdType.MESH


def split_table(table, terms):
    rest = table.astype(np.float32)
    pieces = []
    for _ in range(terms):
        piece = rest.astype(ml_dtypes.bfloat16)
        pieces.append(piece)
        rest = rest - piece.astype(np.float32)
    return pieces


def phase_tables(coef_count):
    coef = np.arange(coef_count)
    kx, ky = coef % IMGBOX - IMGBOX // 2, coef // IMGBOX
    shift = np.arange(64)
    dx, dy = shift % GRID - GRID // 2, shift // GRID - GRID // 2
    turns = (kx[None, :] * dx[:, None] + ky[None, :] * dy[:, None]) % IMGBOX
    angles = turns * (-2.0 * math.pi / IMGBOX)
    return (
        np.concatenate(split_table(np.cos(angles), 3)),
        np.concatenate(split_table(np.sin(angles), 3)),
    )


def dft_tables():
    index = np.arange(BOX)
    angles = (index[:, None] * index[None, :] % BOX) * (2.0 * math.pi / BOX)
    factor = 1.0 / math.sqrt(BOX)
    return np.cos(angles) * factor, np.sin(angles) * factor


def z_tables(block_len, chunks):
    cosine, sine = dft_tables()
    span = BOX // chunks
    full = np.zeros((2, BOX, chunks, 2, span))
    cos_c, sin_c = cosine.reshape(BOX, chunks, span), sine.reshape(BOX, chunks, span)
    full[0, :, :, 0], full[0, :, :, 1] = cos_c, sin_c
    full[1, :, :, 0], full[1, :, :, 1] = -sin_c, cos_c
    full = full.reshape(2, BOX // block_len, block_len, 2 * BOX).transpose(1, 0, 2, 3)
    full = full.reshape(BOX // block_len, 2 * block_len, 2 * BOX)
    return np.stack(split_table(full, 2), axis=1)


def cos_sin_split():
    cosine, sine = dft_tables()
    return np.stack(split_table(cosine, 2) + split_table(sine, 2))


def turn_table(width):
    half = width // 2
    table = np.zeros((width, width), np.float32)
    for j in range(half):
        table[j, half + j] = 1.0
        table[half + j, j] = -1.0
    return table.astype(ml_dtypes.bfloat16)


def dot(left, right):
    return jnp.dot(left, right, preferred_element_type=F32)


def params(**more):
    return pltpu.CompilerParams(vmem_limit_bytes=VMEM_BYTES, **more)


def cost(flops, moved):
    return pl.CostEstimate(flops=flops, bytes_accessed=moved, transcendentals=0)


def aligned_chunk(pick, cos_ref, sin_ref, img_ref):
    cosine = dot(pick, cos_ref[...])
    sine = dot(pick, sin_ref[...])
    real = img_ref[0].astype(F32)
    imag = img_ref[1].astype(F32)
    new_real = (real * cosine - imag * sine).astype(BF16)
    new_imag = (real * sine + imag * cosine).astype(BF16)
    return new_real, new_imag


def score_kernel(
    steps, pick_ref, cos_ref, sin_ref, img_ref, proj_ref, noise_ref, out_ref, aligned_ref, norm
):
    step = pl.program_id(0)
    rows = img_ref.shape[1]
    chunk = img_ref.shape[2]

    @pl.when(step == 0)
    def _():
        out_ref[...] = jnp.zeros_like(out_ref)
        norm[...] = jnp.zeros_like(norm)

    noise = noise_ref[...]
    weighted = []
    for part in range(2):
        proj = proj_ref[part].astype(F32)
        scaled = proj * noise
        weighted.append(scaled.astype(BF16))
        power = scaled * proj
        for lane in range(0, chunk, 128):
            norm[...] += power[:, lane : lane + 128]
    dims = (((1,), (1,)), ((), ()))
    for group in range(pick_ref.shape[0] // rows):
        span = pl.ds(group * rows, rows)
        real, imag = aligned_chunk(pick_ref[span, :], cos_ref, sin_ref, img_ref)
        aligned_ref[0, span, :] = real
        aligned_ref[1, span, :] = imag
        out_ref[span, :] += lax.dot_general(
            real, weighted[0], dims, preferred_element_type=F32
        ) + lax.dot_general(imag, weighted[1], dims, preferred_element_type=F32)

    @pl.when(step == steps - 1)
    def _():
        out_ref[...] -= 0.5 * jnp.sum(norm[...].T, axis=0, keepdims=True)


def slice_kernel(aligned_ref, prob_ref, out_ref):
    block_len = out_ref.shape[3]
    for part in range(2):
        total = dot(prob_ref[...], aligned_ref[part])
        for block in range(out_ref.shape[0]):
            piece = total[:, block * block_len : (block + 1) * block_len]
            out_ref[block, part] = piece.astype(BF16)


def interp_kernel(tables, value_ref, id_ref, table_ref, out_ref):
    group, _, orient, block_len = value_ref.shape
    batch = math.gcd(tables, 8)
    values = value_ref[...].reshape(group * 2 * orient, block_len)
    ids = id_ref[...].reshape(group * 2 * orient, block_len)
    total = jnp.zeros(values.shape, F32)
    for first in range(0, tables, batch):
        picked = [
            jnp.where(ids == jnp.asarray(w, BF16), values, jnp.zeros_like(values))
            for w in range(first, first + batch)
        ]
        total += dot(
            jnp.concatenate(picked, axis=1),
            table_ref[first * block_len : (first + batch) * block_len, :],
        )
    total = total.astype(BF16).reshape(group, 2, orient, block_len)
    for block in range(group):
        for part in range(2):
            lanes = slice(part * block_len, (part + 1) * block_len)
            out_ref[block * orient : (block + 1) * orient, lanes] = total[block, part]


def place_kernel(slot_ref, first_ref, second_ref, out_ref):
    step = pl.program_id(0)
    rows = out_ref.shape[0]
    half = first_ref.shape[0]
    wanted = lax.broadcasted_iota(jnp.int32, (rows, half), 0) + step * rows
    total = jnp.zeros(out_ref.shape, F32)
    for index, ref in enumerate((first_ref, second_ref)):
        slots = slot_ref[:, index * half : (index + 1) * half]
        total += dot(jnp.where(wanted == slots, 1.0, 0.0).astype(BF16), ref[...])
    out_ref[...] = total.astype(BF16)


def transform_kernel(
    n_img,
    n_ori,
    count,
    depth,
    cell_ref,
    term_ref,
    z_ref,
    dft_ref,
    turn_ref,
    out_ref,
    to_img,
    from_img,
    to_ori,
    img_send,
    img_recv,
    ori_send,
    ori_recv,
    own_sem,
):
    my_img, my_ori = lax.axis_index("img"), lax.axis_index("ori")
    _, pencils, width = to_img.shape
    x_span, y_out = to_ori.shape[1], to_ori.shape[2]
    y_span = pencils // x_span
    tall = count * y_span
    tiles = x_span // count
    z_blocks = z_ref.shape[0]
    lag = min(2, tiles)

    barrier = pltpu.get_barrier_semaphore()
    for d in range(1, n_img):
        pl.semaphore_signal(
            barrier, inc=1, device_id={"img": lax.rem(my_img + d, n_img)}, device_id_type=MESH
        )
    for d in range(1, n_ori):
        pl.semaphore_signal(
            barrier, inc=1, device_id={"ori": lax.rem(my_ori + d, n_ori)}, device_id_type=MESH
        )
    pl.semaphore_wait(barrier, n_img + n_ori - 2)

    def rows_of(tile):
        return pl.ds(pl.multiple_of(tile * tall, tall), tall)

    def columns_of(tile):
        return pl.ds(tile * count, count)

    def img_copy(tile, d, slab):
        peer = lax.rem(my_img + d, n_img)
        return pltpu.make_async_remote_copy(
            src_ref=to_img.at[peer, rows_of(tile)],
            dst_ref=from_img.at[slab, rows_of(tile)],
            send_sem=img_send.at[tile, d - 1],
            recv_sem=img_recv.at[tile, d - 1],
            device_id={"img": peer},
            device_id_type=MESH,
        )

    def ori_copy(tile, d, slab):
        peer = lax.rem(my_ori + d, n_ori)
        return pltpu.make_async_remote_copy(
            src_ref=to_ori.at[peer, columns_of(tile)],
            dst_ref=out_ref.at[slab, columns_of(tile)],
            send_sem=ori_send.at[tile, d - 1],
            recv_sem=ori_recv.at[tile, d - 1],
            device_id={"ori": peer},
            device_id_type=MESH,
        )

    def own_copy(tile):
        return pltpu.make_async_copy(
            to_ori.at[my_ori, columns_of(tile)],
            out_ref.at[my_ori, columns_of(tile)],
            own_sem.at[tile],
        )

    def along_z(tile):
        first = (lax.broadcasted_iota(jnp.int32, (tall, depth), 0) + tile * tall) * z_blocks
        result = jnp.zeros((tall, n_img * width), F32)
        for half in range(z_blocks):
            total = jnp.zeros((tall, term_ref.shape[1]), F32)
            for start in range(0, term_ref.shape[0], depth):
                hit = jnp.where(first + half == cell_ref[:, start : start + depth], 1.0, 0.0)
                total += dot(hit.astype(BF16), term_ref[start : start + depth, :])
            total = total.astype(BF16)
            result += dot(total, z_ref[half, 0]) + dot(total, z_ref[half, 1])
        for chunk in range(n_img):
            to_img[chunk, rows_of(tile), :] = result[
                :, chunk * width : (chunk + 1) * width
            ].astype(BF16)
        for d in range(1, n_img):
            img_copy(tile, d, my_img).start()
        from_img[my_img, rows_of(tile), :] = to_img[my_img, rows_of(tile), :]

    def along_y(tile):
        for d in range(1, n_img):
            img_copy(tile, d, lax.rem(my_img - d + n_img, n_img)).wait_recv()
        plain, turned = [], []
        for x in range(count):
            place = pl.ds(pl.multiple_of(tile * tall + x * y_span, y_span), y_span)
            column = jnp.concatenate(
                [from_img[source, place, :] for source in range(n_img)], axis=0
            )
            plain.append(column)
            turned.append(dot(column, turn_ref[...]).astype(BF16))
        plain = jnp.concatenate(plain, axis=1)
        turned = jnp.concatenate(turned, axis=1)
        result = dot(dft_ref[0], plain) + dot(dft_ref[1], plain)
        result += dot(dft_ref[2], turned) + dot(dft_ref[3], turned)
        for x in range(count):
            for target in range(n_ori):
                to_ori[target, tile * count + x] = result[
                    target * y_out : (target + 1) * y_out, x * width : (x + 1) * width
                ].astype(BF16)
        for d in range(1, n_ori):
            ori_copy(tile, d, my_ori).start()
        own_copy(tile).start()

    @pl.loop(0, tiles + lag)
    def _(step):
        @pl.when(step < tiles)
        def _():
            along_z(step)

        @pl.when(step >= lag)
        def _():
            along_y(step - lag)

    @pl.loop(0, tiles)
    def _(tile):
        for d in range(1, n_img):
            img_copy(tile, d, my_img).wait_send()
        for d in range(1, n_ori):
            ori_copy(tile, d, my_ori).wait_send()
            ori_copy(tile, d, lax.rem(my_ori - d + n_ori, n_ori)).wait_recv()
        own_copy(tile).wait()


def x_kernel(dft_ref, in_ref, out_ref, wide, left):
    box, count, width = in_ref.shape
    half = width // 2
    wide[...] = in_ref[...].astype(F32)
    for y in range(count):
        row = wide[:, y, :].T
        left[0, y * width : (y + 1) * width, :] = row.astype(BF16)
        left[1, y * width : (y + 1) * width, :] = jnp.concatenate(
            [-row[half:], row[:half]], axis=0
        ).astype(BF16)
    result = dot(left[0], dft_ref[0]) + dot(left[0], dft_ref[1])
    result += dot(left[1], dft_ref[2]) + dot(left[1], dft_ref[3])
    for y in range(count):
        out_ref[:, y, :] = result[y * width : (y + 1) * width, :]


def whole(shape):
    return pl.BlockSpec(shape, lambda i: (0,) * len(shape))


def combine(pairs):
    peaks, totals = pairs[:, 0], pairs[:, 1]
    peak = jnp.max(peaks, axis=0)
    return peak, jnp.sum(totals * jnp.exp(peaks - peak), axis=0)


def local(
    images, projections, noise_weight, shift_ids, owner_ids, cell_ids, weight_ids, interp_table
):
    n_img, n_ori = lax.axis_size("img"), lax.axis_size("ori")
    devices = n_img * n_ori
    row_count, _, coef_count = images.shape
    shift_count = shift_ids.shape[1]
    orient = projections.shape[0]
    tables, block_len, _ = interp_table.shape
    rows = row_count * shift_count
    blocks = owner_ids.shape[1]
    block_count = orient * blocks
    capacity = max(2, (3 * block_count + devices - 1) // devices)
    slots = devices * capacity

    owners = owner_ids.T.reshape(-1)
    cells = cell_ids.T.reshape(-1)
    group = math.gcd(block_count, 128)
    named = owners[:, None] == jnp.arange(devices, dtype=jnp.int32)[None, :]
    named_b = named.astype(BF16).reshape(-1, group, devices)
    lower = jnp.tril(jnp.ones((group, group), BF16))
    within = jnp.einsum("ij,gjd->gid", lower, named_b, preferred_element_type=F32)
    before = jnp.cumsum(within[:, -1], axis=0) - within[:, -1]
    running = (within + before[:, None, :]).reshape(block_count, devices)
    rank = jnp.sum(jnp.where(named, running, 0.0), axis=1).astype(jnp.int32) - 1
    slot_ids = owners * capacity + rank
    send_cells = (
        jnp.full((slots,), -1, jnp.int32).at[slot_ids].set(cells).reshape(devices, capacity)
    )
    got_cells = lax.all_to_all(
        send_cells, ("img", "ori"), split_axis=0, concat_axis=0, tiled=True
    ).reshape(1, slots)
    ids = jnp.broadcast_to(
        weight_ids.T.astype(BF16)[:, None, :, None], (blocks, 2, orient, block_len)
    )

    chunk = math.gcd(coef_count, 1024)
    steps = coef_count // chunk
    cos_table, sin_table = phase_tables(coef_count)
    depth = cos_table.shape[0]
    pick = (
        shift_ids.T.reshape(-1)[:, None] == jnp.arange(depth, dtype=jnp.int32)[None, :] % 64
    ).astype(BF16)
    image_parts = images.transpose(1, 0, 2)
    proj_parts = projections.transpose(1, 0, 2)
    table_spec = pl.BlockSpec((depth, chunk), lambda i: (0, i))
    image_spec = pl.BlockSpec((2, row_count, chunk), lambda i: (0, 0, i))
    scores, aligned = pl.pallas_call(
        functools.partial(score_kernel, steps),
        grid=(steps,),
        out_shape=(
            jax.ShapeDtypeStruct((rows, orient), F32),
            jax.ShapeDtypeStruct((2, rows, coef_count), BF16),
        ),
        in_specs=[
            whole((rows, depth)),
            table_spec,
            table_spec,
            image_spec,
            pl.BlockSpec((2, orient, chunk), lambda i: (0, 0, i)),
            pl.BlockSpec((1, chunk), lambda i: (0, i)),
        ],
        out_specs=(
            whole((rows, orient)),
            pl.BlockSpec((2, rows, chunk), lambda i: (0, 0, i)),
        ),
        scratch_shapes=[pltpu.VMEM((orient, 128), F32)],
        compiler_params=params(),
        name="scores",
    )(pick, cos_table, sin_table, image_parts, proj_parts, noise_weight.reshape(1, -1))
    scores = scores.reshape(shift_count, row_count, orient)
    local_peak = jnp.max(scores, axis=(0, 2))
    local_total = jnp.sum(jnp.exp(scores - local_peak[None, :, None]), axis=(0, 2))
    peak, total = combine(lax.all_gather(jnp.stack([local_peak, local_total]), "ori"))
    loglik = peak + jnp.log(total)
    prob = (jnp.exp(scores - peak[None, :, None]) / total[None, :, None]).astype(BF16)
    prob = prob.reshape(rows, orient).T

    half_blocks = blocks // 2
    half_chunk = half_blocks * block_len
    half_count = half_blocks * orient
    half_shape = (n_img * half_blocks, 2, orient, block_len)
    group = math.gcd(half_blocks, 4)
    group_shape = (group, 2, orient, block_len)
    flat_table = interp_table.reshape(tables * block_len, block_len)
    halves = []
    for half in range(2):
        partial_sums = pl.pallas_call(
            slice_kernel,
            grid=(n_img,),
            out_shape=jax.ShapeDtypeStruct(half_shape, BF16),
            in_specs=[
                pl.BlockSpec((2, rows, half_chunk), lambda i, half=half: (0, 0, 2 * i + half)),
                whole((orient, rows)),
            ],
            out_specs=pl.BlockSpec((half_blocks, 2, orient, block_len), lambda i: (i, 0, 0, 0)),
            compiler_params=params(),
            cost_estimate=cost(2 * orient * rows * coef_count, 2 * rows * coef_count),
            name="slices",
        )(aligned, prob)
        halves.append(lax.psum_scatter(partial_sums, "img", scatter_dimension=0, tiled=True))
    terms = []
    for half in range(2):
        offset = half * (half_blocks // group)
        terms.append(
            pl.pallas_call(
                functools.partial(interp_kernel, tables),
                grid=(half_blocks // group,),
                out_shape=jax.ShapeDtypeStruct((half_count, 2 * block_len), BF16),
                in_specs=[
                    pl.BlockSpec(group_shape, lambda i: (i, 0, 0, 0)),
                    pl.BlockSpec(group_shape, lambda i, offset=offset: (i + offset, 0, 0, 0)),
                    whole(flat_table.shape),
                ],
                out_specs=pl.BlockSpec((group * orient, 2 * block_len), lambda i: (i, 0)),
                compiler_params=params(),
                cost_estimate=cost(
                    8 * half_count * tables * block_len * block_len, 4 * half_count * block_len
                ),
                name="interpolate",
            )(halves[half], ids, flat_table)
        )

    tile = math.gcd(slots, 512)
    send_terms = pl.pallas_call(
        place_kernel,
        grid=(slots // tile,),
        out_shape=jax.ShapeDtypeStruct((slots, 2 * block_len), BF16),
        in_specs=[whole((1, block_count))] + [whole((half_count, 2 * block_len))] * 2,
        out_specs=pl.BlockSpec((tile, 2 * block_len), lambda i: (i, 0)),
        compiler_params=params(),
        name="place",
    )(slot_ids.reshape(1, block_count), *terms)
    got_terms = lax.all_to_all(
        send_terms.reshape(devices, capacity, 2 * block_len),
        ("img", "ori"),
        split_axis=0,
        concat_axis=0,
        tiled=True,
    ).reshape(slots, 2 * block_len)

    x_span, y_span, y_out = BOX // n_ori, BOX // n_img, BOX // n_ori
    pencils = x_span * y_span
    width = 2 * (BOX // n_img)
    z_table = z_tables(block_len, n_img)
    dft = cos_sin_split()
    count = math.gcd(x_span, 4)
    tiles = x_span // count
    vmem = pl.BlockSpec(memory_space=pltpu.VMEM)
    pencil_parts = pl.pallas_call(
        functools.partial(transform_kernel, n_img, n_ori, count, math.gcd(slots, 2048)),
        out_shape=jax.ShapeDtypeStruct((n_ori, x_span, y_out, width), BF16),
        in_specs=[vmem] * 5,
        out_specs=pl.BlockSpec(memory_space=pl.ANY),
        scratch_shapes=[
            pltpu.VMEM((n_img, pencils, width), BF16),
            pltpu.VMEM((n_img, pencils, width), BF16),
            pltpu.VMEM((n_ori, x_span, y_out, width), BF16),
            pltpu.SemaphoreType.DMA((tiles, n_img - 1)),
            pltpu.SemaphoreType.DMA((tiles, n_img - 1)),
            pltpu.SemaphoreType.DMA((tiles, n_ori - 1)),
            pltpu.SemaphoreType.DMA((tiles, n_ori - 1)),
            pltpu.SemaphoreType.DMA((tiles,)),
        ],
        compiler_params=params(collective_id=0, has_side_effects=True),
        name="transform",
    )(got_cells, got_terms, z_table, dft, turn_table(width))

    count = math.gcd(y_out, 16)
    realspace = pl.pallas_call(
        x_kernel,
        grid=(y_out // count,),
        out_shape=jax.ShapeDtypeStruct((width, y_out, BOX), F32),
        in_specs=[
            whole(dft.shape),
            pl.BlockSpec((BOX, count, width), lambda i: (0, i, 0)),
        ],
        out_specs=pl.BlockSpec((width, count, BOX), lambda i: (0, i, 0)),
        scratch_shapes=[
            pltpu.VMEM((BOX, count, width), F32),
            pltpu.VMEM((2, count * width, BOX), BF16),
        ],
        compiler_params=params(),
        name="along_x",
    )(dft, pencil_parts.reshape(BOX, y_out, width))
    return realspace.reshape(2, width // 2, y_out, BOX), loglik


def solution(mesh):
    placed = (
        P("img", None, None),
        P("ori", None, None),
        P(),
        P("img", None),
        P("ori", "img"),
        P("ori", "img"),
        P("ori", "img"),
        P(),
    )
    return jax.shard_map(
        local,
        mesh=mesh,
        in_specs=placed,
        out_specs=(P(None, "img", "ori", None), P("img")),
        check_vma=False,
    )
```

time: 393 us -> 338 us (0.86)
  waiting for transfers between devices: 158 us -> 109 us
  blocking collectives: 44.3 us -> 14.4 us
  Pallas kernels: 124 us -> 153 us
    all_to_all x1 -> x0, waiting for transfers between devices: 48.4 us -> none  [local(): lax.all_to_all(pencil_parts, 'ori', split_axis=0, concat_axis=0, tiled=True)]
    all_to_all x1 -> x0, blocking collectives: 29.9 us -> none  [local(): lax.all_to_all(pencil_parts, 'img', split_axis=0, concat_axis=0, tiled=True)]
    pallas_call x4 -> x6, Pallas kernels: 83.9 us -> 110 us  [the longest x1 58.8 us: local(): pl.pallas_call(functools.partial(transform_kernel, n_img, n_ori, count, m...]
    unnamed x23 -> x21, local copies, waits for them, and re-layouts: 21 us -> 19 us
    reduce_scatter x1 -> x2, waiting for transfers between devices: 37.6 us -> 38 us  [local(): lax.psum_scatter(partial_sums, 'img', scatter_dimension=0, tiled=True)]
  transfers between devices with their start and end apart: 4 -> 4, of which waited for: 3 -> 3; matrix products, arithmetic and copies ran while one was open for 3% -> 4% of each run, Pallas kernels for 8% -> 13%
where the time goes in v1:
time: 338 us; the launch traced here: 337 us
  Pallas kernels  153 us (45%)
  waiting for transfers between devices  109 us (32%)
  local copies, waits for them, and re-layouts  31.7 us (9%)
  blocking collectives  14.4 us (4%)
  between operations  14.3 us (4%)
  starting transfers between devices  9.23 us (3%)
  other arithmetic  5.68 us (2%)
    all_to_all x1, waiting for transfers between devices, local(): lax.all_to_all(send_terms.reshape(devices, capacity, 2 * block_len), ('im...  71 us
    pallas_call x1, Pallas kernels, local(): pl.pallas_call(functools.partial(transform_kernel, n_img, n_ori, count, m...  58.8 us
    reduce_scatter x2, waiting for transfers between devices, local(): lax.psum_scatter(partial_sums, 'img', scatter_dimension=0, tiled=True)  38 us
    pallas_call x1, Pallas kernels, local(): pl.pallas_call(functools.partial(score_kernel, steps), grid=(steps,), out...  34.3 us
    pallas_call x2, Pallas kernels, local(): pl.pallas_call(functools.partial(interp_kernel, tables), grid=(half_block...  23 us
    unnamed x21, local copies, waits for them, and re-layouts  19 us
    pallas_call x2, Pallas kernels, local(): pl.pallas_call(slice_kernel, grid=(n_img,), out_shape=jax.ShapeDtypeStruc...  17.2 us
    all_gather x1, blocking collectives, local(): lax.all_gather(jnp.stack([local_peak, local_total]), 'ori')  14.4 us
  transfers between devices with their start and end apart: 4, of which 3 were waited for; matrix products, arithmetic and copies ran while one was open for 4% of the time, Pallas kernels for 13%

profile of v1, /device:TPU:0, one launch (start us, length us, event | category | flops | bytes accessed | tf_op | source)
XLA Modules:
  0.0 337.1 jit_solution(6315226911876970542)
XLA Ops:
  7.2 0.0 reduce-scatter.5.cloned.1.call-start
  7.2 0.0 copy-start.1
  7.2 12.7 %copy.53 = bf16[256,2,8192]{2,0,1:T(8,128)(2,1)} copy(bf16[256,2,8192]{2,1,0:T(2,128)(2,1)} %param.13) | data formatting | bytes 16777216 | tf_op args[0]
  19.9 0.0 copy-done.1
  19.9 0.0 copy-start.5
  19.9 4.6 %copy.54 = bf16[128,2,8192]{2,0,1:T(8,128)(2,1)} copy(bf16[128,2,8192]{2,1,0:T(2,128)(2,1)S(1)} %copy-done.1) | data formatting | bytes 8388608 | tf_op args[1]
  24.5 0.0 copy-done.5
  24.5 1.0 compare_convert_fusion.pick_ref
  25.5 34.3 %scores.1 = (f32[1024,128]{1,0:T(8,128)}, bf16[2,1024,8192]{2,1,0:T(8,128)(2,1)}) custom-call(bf16[1024,192]{1,0:T(8,128)(2,1)} %compare_convert_fusion.pick_ref, bf16[192,8192]{1,0:T(8,128)(2,1)} %constant.47.clone.cos_ref, bf16[192,8192]{1,0:T(8,128)(2,1)} %constant.48.clone.sin_ref, bf16[2,256,8192]{2,1,0:T(8,128)(2,1)} %bitcast.58, ...), custom_call_target="tpu_custom_call" | custom-call | tf_op jit(solution)/shard_map/scores/pallas_call | solution.py:389
  59.9 1.2 copy.37
  61.1 1.2 reduce_max.21
  62.4 1.4 exponential_reduce_fusion
  63.9 14.4 %all-gather.1 = f32[8,2,256]{2,1,0:T(2,128)S(1)} all-gather(f32[1,2,256]{2,1,0:T(2,128)S(1)} %maximum_bitcast_fusion), channel_id=2, replica_groups=mesh['img'=4,'ori'=8] {'ori'}, dimensions={0}, use_global_device_ids=true | all-gather | bytes 18432 | tf_op jit(solution)/shard_map/all_gather | solution.py:415
  78.3 0.8 fusion.prob_ref
  79.1 8.5 %slices.3 = bf16[32,2,128,128]{3,2,1,0:T(8,128)(2,1)} custom-call(bf16[2,1024,8192]{2,1,0:T(8,128)(2,1)} %get-tuple-element.4.aligned_ref, bf16[128,1024]{1,0:T(8,128)(2,1)} %fusion.prob_ref), custom_call_target="tpu_custom_call" | custom-call | flops 2147483648 | bytes 16777216 | tf_op jit(solution)/shard_map/slices/pallas_call | solution.py:429
  87.6 0.0 reduce-scatter.5.cloned.1.call-update
  87.6 0.0 copy-start.3
  87.6 0.0 reduce-scatter.3.cloned.1.call-start
  87.7 8.8 %slices.2 = bf16[32,2,128,128]{3,2,1,0:T(8,128)(2,1)} custom-call(bf16[2,1024,8192]{2,1,0:T(8,128)(2,1)} %get-tuple-element.4.aligned_ref, bf16[128,1024]{1,0:T(8,128)(2,1)} %fusion.prob_ref), custom_call_target="tpu_custom_call" | custom-call | flops 2147483648 | bytes 16777216 | tf_op jit(solution)/shard_map/slices/pallas_call | solution.py:429
  96.5 0.0 reduce-scatter.3.cloned.1.call-update
  96.5 0.0 copy-done.3
  96.5 0.2 convolution_bitcast_fusion
  96.7 0.1 slice.13
  96.8 0.2 copy.33
  97.0 0.2 copy.34
  97.2 0.3 subtract_reduce_fusion
  97.5 0.1 select_reduce_fusion
  97.6 0.0 copy-start.2
  97.7 8.2 %scatter_custom_fusion = s32[6144]{0:T(1024)S(1)} fusion(s32[2048]{0:T(1024)S(1)} %bitcast.74, s32[2048]{0:T(1024)} %bitcast.79, s32[]{:T(128)} %constant.20.clone.1), kind=kCustom, calls=%fused_computation.18 | custom fusion | bytes 25088 | tf_op jit(solution)/shard_map/scatter | solution.py:369
  105.9 0.7 all_to_all.9
  106.6 4.3 %all-to-all-start = ((s32[32,1,192]{2,1,0:T(1,128)}), s32[32,1,192]{2,1,0:T(1,128)S(1)}, u32[]{:S(2)}, u32[]{:S(2)}) async-start(s32[32,1,192]{2,1,0:T(1,128)} %all_to_all.9), calls=%async_computation | async-start | bytes 65536 | tf_op jit(solution)/shard_map/all_to_all | solution.py:371
  110.9 0.0 copy-done.4
  111.0 12.0 %reduce-scatter.5.cloned.1.call-done.value_ref = bf16[8,2,128,128]{3,2,1,0:T(8,128)(2,1)} async-done(((bf16[32,2,128,128]{3,2,1,0:T(8,128)(2,1)}), bf16[8,2,128,128]{3,2,1,0:T(8,128)(2,1)}) %reduce-scatter.5.cloned.1.call-update) | async-done | bytes 524304 | tf_op jit(solution)/shard_map/reduce_scatter | solution.py:442
  122.9 1.4 broadcast_in_dim.32.id_ref
  124.3 11.5 %interpolate.3.second_ref = bf16[1024,256]{1,0:T(8,128)(2,1)} custom-call(bf16[8,2,128,128]{3,2,1,0:T(8,128)(2,1)} %reduce-scatter.5.cloned.1.call-done.value_ref, bf16[16,2,128,128]{3,2,1,0:T(8,128)(2,1)} %broadcast_in_dim.32.id_ref, bf16[8192,128]{1,0:T(8,128)(2,1)} %bitcast.77), custom_call_target="tpu_custom_call" | custom-call | flops 8589934592 | bytes 524288 | tf_op jit(solution)/shard_map/interpolate/pallas_call | solution.py:447
  135.8 0.0 copy-done.2
  135.8 26.0 %reduce-scatter.3.cloned.1.call-done.value_ref = bf16[8,2,128,128]{3,2,1,0:T(8,128)(2,1)} async-done(((bf16[32,2,128,128]{3,2,1,0:T(8,128)(2,1)}), bf16[8,2,128,128]{3,2,1,0:T(8,128)(2,1)}) %reduce-scatter.3.cloned.1.call-update) | async-done | bytes 524304 | tf_op jit(solution)/shard_map/reduce_scatter | solution.py:442
  161.8 11.5 %interpolate.2.first_ref = bf16[1024,256]{1,0:T(8,128)(2,1)} custom-call(bf16[8,2,128,128]{3,2,1,0:T(8,128)(2,1)} %reduce-scatter.3.cloned.1.call-done.value_ref, bf16[16,2,128,128]{3,2,1,0:T(8,128)(2,1)} %broadcast_in_dim.32.id_ref, bf16[8192,128]{1,0:T(8,128)(2,1)} %bitcast.78), custom_call_target="tpu_custom_call" | custom-call | flops 8589934592 | bytes 524288 | tf_op jit(solution)/shard_map/interpolate/pallas_call | solution.py:447
  173.3 10.6 %place.1 = bf16[6144,256]{1,0:T(8,128)(2,1)} custom-call(s32[1,2048]{1,0:T(1,128)} %bitcast.65, bf16[1024,256]{1,0:T(8,128)(2,1)} %interpolate.2.first_ref, bf16[1024,256]{1,0:T(8,128)(2,1)} %interpolate.3.second_ref), custom_call_target="tpu_custom_call" | custom-call | tf_op jit(solution)/shard_map/place/pallas_call | solution.py:466
  183.9 0.0 all-to-all-done
  183.9 4.8 %all-to-all-start.1 = ((bf16[32,192,256]{2,1,0:T(8,128)(2,1)}), bf16[32,192,256]{2,1,0:T(8,128)(2,1)S(1)}, u32[]{:S(2)}, u32[]{:S(2)}) async-start(bf16[32,192,256]{2,1,0:T(8,128)(2,1)} %bitcast.60), calls=%async_computation.3 | async-start | bytes 6291456 | tf_op jit(solution)/shard_map/all_to_all | solution.py:475
  188.8 0.6 log_add_fusion
  189.3 0.1 reduce.7
  189.4 0.7 reshape.166.cell_ref
  190.1 71.0 %all-to-all-done.1 = bf16[32,192,256]{2,1,0:T(8,128)(2,1)S(1)} async-done(((bf16[32,192,256]{2,1,0:T(8,128)(2,1)}), bf16[32,192,256]{2,1,0:T(8,128)(2,1)S(1)}, u32[]{:S(2)}, u32[]{:S(2)}) %all-to-all-start.1) | async-done | bytes 3145760 | tf_op jit(solution)/shard_map/all_to_all | solution.py:475
  261.1 1.7 copy-done
  262.8 58.8 %transform.1 = bf16[8,32,32,128]{3,2,1,0:T(8,128)(2,1)} custom-call(s32[1,6144]{1,0:T(1,128)} %reshape.166.cell_ref, bf16[6144,256]{1,0:T(8,128)(2,1)} %bitcast.61, bf16[2,2,256,512]{3,2,1,0:T(8,128)(2,1)} %constant.49.clone.z_ref, bf16[4,256,256]{2,1,0:T(8,128)(2,1)} %constant.50.clone.dft_ref, bf16[128,128]{1,0:T(8,128)(2,1)} %constant.51.clone.turn_ref), custom_call_target="tpu_custom_call" | custom-call | tf_op jit(solution)/shard_map/transform/pallas_call | solution.py:491
  321.6 8.7 %along_x.1 = f32[128,32,256]{2,1,0:T(8,128)} custom-call(bf16[4,256,256]{2,1,0:T(8,128)(2,1)} %constant.50.clone.dft_ref, bf16[256,32,128]{2,1,0:T(8,128)(2,1)} %bitcast.62), custom_call_target="tpu_custom_call" | custom-call | tf_op jit(solution)/shard_map/along_x/pallas_call | solution.py:511
  (21 shorter events, 0.2 us)
Async XLA Ops:
  7.2 115.7 %reduce-scatter.5.cloned.1.call-start = ((), (), s32[]{:S(2)}) async-start(), calls=%async_computation.5 | async-start | bytes 2621440 | tf_op jit(solution)/shard_map/reduce_scatter | solution.py:442
  7.2 12.7 %copy-start.1 = (bf16[128,2,8192]{2,1,0:T(2,128)(2,1)S(1)}, bf16[128,2,8192]{2,1,0:T(2,128)(2,1)}, u32[]{:S(2)}) copy-start(bf16[128,2,8192]{2,1,0:T(2,128)(2,1)} %param.14) | copy-start | bytes 12582916
  19.9 4.6 %copy-start.5 = (s32[256,4]{0,1:T(4,128)S(1)}, s32[256,4]{0,1:T(4,128)}, u32[]{:S(2)}) copy-start(s32[256,4]{0,1:T(4,128)} %param.16) | copy-start | bytes 12292
  87.6 8.9 %copy-start.3 = (s32[128,16]{0,1:T(8,128)S(1)}, s32[128,16]{0,1:T(8,128)}, u32[]{:S(2)}) copy-start(s32[128,16]{0,1:T(8,128)} %param.17) | copy-start | bytes 24580
  87.6 74.2 %reduce-scatter.3.cloned.1.call-start = ((), (), s32[]{:S(2)}) async-start(), calls=%async_computation.4 | async-start | bytes 2621440 | tf_op jit(solution)/shard_map/reduce_scatter | solution.py:442
  96.5 14.5 %copy-start.4 = (s32[128,16]{0,1:T(8,128)S(1)}, s32[128,16]{0,1:T(8,128)}, u32[]{:S(2)}) copy-start(s32[128,16]{0,1:T(8,128)} %param.19) | copy-start | bytes 24580
  97.6 38.1 %copy-start.2 = (s32[16,128]{1,0:T(8,128)}, s32[16,128]{1,0:T(8,128)S(1)}, u32[]{:S(2)}) copy-start(s32[16,128]{1,0:T(8,128)S(1)} %add_add_fusion) | copy-start | bytes 24580
  106.6 77.3 %all-to-all-start = ((s32[32,1,192]{2,1,0:T(1,128)}), s32[32,1,192]{2,1,0:T(1,128)S(1)}, u32[]{:S(2)}, u32[]{:S(2)}) async-start(s32[32,1,192]{2,1,0:T(1,128)} %all_to_all.9), calls=%async_computation | async-start | bytes 65536 | tf_op jit(solution)/shard_map/all_to_all | solution.py:371
  183.9 77.2 %all-to-all-start.1 = ((bf16[32,192,256]{2,1,0:T(8,128)(2,1)}), bf16[32,192,256]{2,1,0:T(8,128)(2,1)S(1)}, u32[]{:S(2)}, u32[]{:S(2)}) async-start(bf16[32,192,256]{2,1,0:T(8,128)(2,1)} %bitcast.60), calls=%async_computation.3 | async-start | bytes 6291456 | tf_op jit(solution)/shard_map/all_to_all | solution.py:475
  261.1 1.7 copy-start
Sparse Core Ops, SparseCore 0:
  87.8 35.1 reduce-scatter.4
  126.7 35.0 reduce-scatter.2

commit v2 on v1

--- a/solution.py
+++ b/solution.py
@@ -81,10 +81,6 @@
 
 def params(**more):
     return pltpu.CompilerParams(vmem_limit_bytes=VMEM_BYTES, **more)
-
-
-def cost(flops, moved):
-    return pl.CostEstimate(flops=flops, bytes_accessed=moved, transcendentals=0)
 
 
 def aligned_chunk(pick, cos_ref, sin_ref, img_ref):
@@ -133,47 +129,97 @@
         out_ref[...] -= 0.5 * jnp.sum(norm[...].T, axis=0, keepdims=True)
 
 
-def slice_kernel(aligned_ref, prob_ref, out_ref):
-    block_len = out_ref.shape[3]
+def slice_kernel(
+    n_img,
+    subs,
+    tables,
+    aligned_ref,
+    prob_ref,
+    id_ref,
+    table_ref,
+    out_ref,
+    to_peer,
+    from_peer,
+    send_sem,
+    recv_sem,
+):
+    step = pl.program_id(0)
+    sub, target = step // n_img, step % n_img
+    me = lax.axis_index("img")
+    _, _, group, _, orient, block_len = to_peer.shape
+
+    @pl.when(step == 0)
+    def _():
+        barrier = pltpu.get_barrier_semaphore()
+        for d in range(1, n_img):
+            pl.semaphore_signal(
+                barrier, inc=1, device_id={"img": lax.rem(me + d, n_img)}, device_id_type=MESH
+            )
+        pl.semaphore_wait(barrier, n_img - 1)
+
+    def peer_copy(part_index, peer, slab):
+        return pltpu.make_async_remote_copy(
+            src_ref=to_peer.at[part_index, peer],
+            dst_ref=from_peer.at[part_index, slab],
+            send_sem=send_sem.at[part_index, peer],
+            recv_sem=recv_sem.at[part_index, slab],
+            device_id={"img": peer},
+            device_id_type=MESH,
+        )
+
     for part in range(2):
         total = dot(prob_ref[...], aligned_ref[part])
-        for block in range(out_ref.shape[0]):
+        for block in range(group):
             piece = total[:, block * block_len : (block + 1) * block_len]
-            out_ref[block, part] = piece.astype(BF16)
-
-
-def interp_kernel(tables, value_ref, id_ref, table_ref, out_ref):
-    group, _, orient, block_len = value_ref.shape
-    batch = math.gcd(tables, 8)
-    values = value_ref[...].reshape(group * 2 * orient, block_len)
-    ids = id_ref[...].reshape(group * 2 * orient, block_len)
-    total = jnp.zeros(values.shape, F32)
-    for first in range(0, tables, batch):
-        picked = [
-            jnp.where(ids == jnp.asarray(w, BF16), values, jnp.zeros_like(values))
-            for w in range(first, first + batch)
-        ]
-        total += dot(
-            jnp.concatenate(picked, axis=1),
-            table_ref[first * block_len : (first + batch) * block_len, :],
-        )
-    total = total.astype(BF16).reshape(group, 2, orient, block_len)
-    for block in range(group):
-        for part in range(2):
-            lanes = slice(part * block_len, (part + 1) * block_len)
-            out_ref[block * orient : (block + 1) * orient, lanes] = total[block, part]
-
-
-def place_kernel(slot_ref, first_ref, second_ref, out_ref):
+            to_peer[sub, target, block, part] = piece.astype(BF16)
+
+    @pl.when(target != me)
+    def _():
+        peer_copy(sub, target, me).start()
+
+    @pl.when(step == subs * n_img - 1)
+    def _():
+        @pl.loop(0, subs)
+        def _(index):
+            from_peer[index, me] = to_peer[index, me]
+            for d in range(1, n_img):
+                source = lax.rem(me + d, n_img)
+                peer_copy(index, source, source).wait_recv()
+            summed = from_peer[index, 0].astype(F32)
+            for source in range(1, n_img):
+                summed += from_peer[index, source].astype(F32)
+            values = summed.astype(BF16).reshape(group * 2 * orient, block_len)
+            ids = id_ref[pl.ds(index * group, group)].reshape(group * 2 * orient, block_len)
+            batch = math.gcd(tables, 8)
+            total = jnp.zeros(values.shape, F32)
+            for first in range(0, tables, batch):
+                picked = [
+                    jnp.where(ids == jnp.asarray(w, BF16), values, jnp.zeros_like(values))
+                    for w in range(first, first + batch)
+                ]
+                total += dot(
+                    jnp.concatenate(picked, axis=1),
+                    table_ref[first * block_len : (first + batch) * block_len, :],
+                )
+            total = total.astype(BF16).reshape(group, 2, orient, block_len)
+            for block in range(group):
+                place = pl.multiple_of((index * group + block) * orient, orient)
+                for part in range(2):
+                    lanes = slice(part * block_len, (part + 1) * block_len)
+                    out_ref[pl.ds(place, orient), lanes] = total[block, part]
+
+        @pl.loop(0, subs)
+        def _(index):
+            for d in range(1, n_img):
+                peer_copy(index, lax.rem(me + d, n_img), me).wait_send()
+
+
+def place_kernel(slot_ref, term_ref, out_ref):
     step = pl.program_id(0)
     rows = out_ref.shape[0]
-    half = first_ref.shape[0]
-    wanted = lax.broadcasted_iota(jnp.int32, (rows, half), 0) + step * rows
-    total = jnp.zeros(out_ref.shape, F32)
-    for index, ref in enumerate((first_ref, second_ref)):
-        slots = slot_ref[:, index * half : (index + 1) * half]
-        total += dot(jnp.where(wanted == slots, 1.0, 0.0).astype(BF16), ref[...])
-    out_ref[...] = total.astype(BF16)
+    wanted = lax.broadcasted_iota(jnp.int32, (rows, term_ref.shape[0]), 0) + step * rows
+    hit = jnp.where(wanted == slot_ref[...], 1.0, 0.0).astype(BF16)
+    out_ref[...] = dot(hit, term_ref[...]).astype(BF16)
 
 
 def transform_kernel(
@@ -368,9 +414,6 @@
     send_cells = (
         jnp.full((slots,), -1, jnp.int32).at[slot_ids].set(cells).reshape(devices, capacity)
     )
-    got_cells = lax.all_to_all(
-        send_cells, ("img", "ori"), split_axis=0, concat_axis=0, tiled=True
-    ).reshape(1, slots)
     ids = jnp.broadcast_to(
         weight_ids.T.astype(BF16)[:, None, :, None], (blocks, 2, orient, block_len)
     )
@@ -412,66 +455,55 @@
     scores = scores.reshape(shift_count, row_count, orient)
     local_peak = jnp.max(scores, axis=(0, 2))
     local_total = jnp.sum(jnp.exp(scores - local_peak[None, :, None]), axis=(0, 2))
-    peak, total = combine(lax.all_gather(jnp.stack([local_peak, local_total]), "ori"))
+    pairs = lax.all_gather(jnp.stack([local_peak, local_total]), "ori")
+    pairs, send_cells, slot_ids, ids = lax.optimization_barrier(
+        (pairs, send_cells, slot_ids, ids)
+    )
+    got_cells = lax.all_to_all(
+        send_cells, ("img", "ori"), split_axis=0, concat_axis=0, tiled=True
+    ).reshape(1, slots)
+    peak, total = combine(pairs)
     loglik = peak + jnp.log(total)
     prob = (jnp.exp(scores - peak[None, :, None]) / total[None, :, None]).astype(BF16)
     prob = prob.reshape(rows, orient).T
 
-    half_blocks = blocks // 2
-    half_chunk = half_blocks * block_len
-    half_count = half_blocks * orient
-    half_shape = (n_img * half_blocks, 2, orient, block_len)
-    group = math.gcd(half_blocks, 4)
-    group_shape = (group, 2, orient, block_len)
+    group = math.gcd(blocks, 4)
+    subs = blocks // group
     flat_table = interp_table.reshape(tables * block_len, block_len)
-    halves = []
-    for half in range(2):
-        partial_sums = pl.pallas_call(
-            slice_kernel,
-            grid=(n_img,),
-            out_shape=jax.ShapeDtypeStruct(half_shape, BF16),
-            in_specs=[
-                pl.BlockSpec((2, rows, half_chunk), lambda i, half=half: (0, 0, 2 * i + half)),
-                whole((orient, rows)),
-            ],
-            out_specs=pl.BlockSpec((half_blocks, 2, orient, block_len), lambda i: (i, 0, 0, 0)),
-            compiler_params=params(),
-            cost_estimate=cost(2 * orient * rows * coef_count, 2 * rows * coef_count),
-            name="slices",
-        )(aligned, prob)
-        halves.append(lax.psum_scatter(partial_sums, "img", scatter_dimension=0, tiled=True))
-    terms = []
-    for half in range(2):
-        offset = half * (half_blocks // group)
-        terms.append(
-            pl.pallas_call(
-                functools.partial(interp_kernel, tables),
-                grid=(half_blocks // group,),
-                out_shape=jax.ShapeDtypeStruct((half_count, 2 * block_len), BF16),
-                in_specs=[
-                    pl.BlockSpec(group_shape, lambda i: (i, 0, 0, 0)),
-                    pl.BlockSpec(group_shape, lambda i, offset=offset: (i + offset, 0, 0, 0)),
-                    whole(flat_table.shape),
-                ],
-                out_specs=pl.BlockSpec((group * orient, 2 * block_len), lambda i: (i, 0)),
-                compiler_params=params(),
-                cost_estimate=cost(
-                    8 * half_count * tables * block_len * block_len, 4 * half_count * block_len
-                ),
-                name="interpolate",
-            )(halves[half], ids, flat_table)
-        )
+    exchange = (subs, n_img, group, 2, orient, block_len)
+    terms = pl.pallas_call(
+        functools.partial(slice_kernel, n_img, subs, tables),
+        grid=(subs * n_img,),
+        out_shape=jax.ShapeDtypeStruct((block_count, 2 * block_len), BF16),
+        in_specs=[
+            pl.BlockSpec(
+                (2, rows, group * block_len), lambda i: (0, 0, i % n_img * subs + i // n_img)
+            ),
+            whole((orient, rows)),
+            whole(ids.shape),
+            whole(flat_table.shape),
+        ],
+        out_specs=whole((block_count, 2 * block_len)),
+        scratch_shapes=[
+            pltpu.VMEM(exchange, BF16),
+            pltpu.VMEM(exchange, BF16),
+            pltpu.SemaphoreType.DMA((subs, n_img)),
+            pltpu.SemaphoreType.DMA((subs, n_img)),
+        ],
+        compiler_params=params(collective_id=1, has_side_effects=True),
+        name="slices",
+    )(aligned, prob, ids, flat_table)
 
     tile = math.gcd(slots, 512)
     send_terms = pl.pallas_call(
         place_kernel,
         grid=(slots // tile,),
         out_shape=jax.ShapeDtypeStruct((slots, 2 * block_len), BF16),
-        in_specs=[whole((1, block_count))] + [whole((half_count, 2 * block_len))] * 2,
+        in_specs=[whole((1, block_count)), whole((block_count, 2 * block_len))],
         out_specs=pl.BlockSpec((tile, 2 * block_len), lambda i: (i, 0)),
         compiler_params=params(),
         name="place",
-    )(slot_ids.reshape(1, block_count), *terms)
+    )(slot_ids.reshape(1, block_count), terms)
     got_terms = lax.all_to_all(
         send_terms.reshape(devices, capacity, 2 * block_len),
         ("img", "ori"),

time: 338 us -> 306 us (0.905)
  waiting for transfers between devices: 109 us -> 71.3 us
  Pallas kernels: 153 us -> 170 us
  between operations: 14.3 us -> 0.86 us
    reduce_scatter x2 -> x0, waiting for transfers between devices: 38 us -> none  [local(): lax.psum_scatter(partial_sums, 'img', scatter_dimension=0, tiled=True)]
    pallas_call x4 -> x1, Pallas kernels: 40.3 us -> 57.6 us  [local(): pl.pallas_call(functools.partial(slice_kernel, n_img, subs, tables), grid...]
    unnamed x21 -> x23, local copies, waits for them, and re-layouts: 19 us -> 19 us
  transfers between devices with their start and end apart: 4 -> 2, of which waited for: 3 -> 1; matrix products, arithmetic and copies ran while one was open for 4% -> 1% of each run, Pallas kernels for 13% -> 22%
where the time goes in v2:
time: 306 us; the launch traced here: 305 us
  Pallas kernels  170 us (56%)
  waiting for transfers between devices  71.3 us (23%)
  local copies, waits for them, and re-layouts  30.7 us (10%)
  blocking collectives  14.4 us (5%)
  starting transfers between devices  12.1 us (4%)
  other arithmetic  5.72 us (2%)
    all_to_all x1, waiting for transfers between devices, local(): lax.all_to_all(send_terms.reshape(devices, capacity, 2 * block_len), ('im...  71.3 us
    pallas_call x1, Pallas kernels, local(): pl.pallas_call(functools.partial(transform_kernel, n_img, n_ori, count, m...  58.8 us
    pallas_call x1, Pallas kernels, local(): pl.pallas_call(functools.partial(slice_kernel, n_img, subs, tables), grid...  57.6 us
    pallas_call x1, Pallas kernels, local(): pl.pallas_call(functools.partial(score_kernel, steps), grid=(steps,), out...  34.5 us
    unnamed x23, local copies, waits for them, and re-layouts  19 us
    all_gather x1, blocking collectives, local(): pairs = lax.all_gather(jnp.stack([local_peak, local_total]), 'ori')  14.4 us
    pallas_call x1, Pallas kernels, local(): pl.pallas_call(place_kernel, grid=(slots // tile,), out_shape=jax.ShapeDt...  10.6 us
    pallas_call x1, Pallas kernels, local(): pl.pallas_call(x_kernel, grid=(y_out // count,), out_shape=jax.ShapeDtype...  8.73 us
  transfers between devices with their start and end apart: 2, of which 1 were waited for; matrix products, arithmetic and copies ran while one was open for 1% of the time, Pallas kernels for 22%

profile of v2, /device:TPU:0, one launch (start us, length us, event | category | flops | bytes accessed | tf_op | source)
XLA Modules:
  0.0 305.4 jit_solution(13758708374150713385)
XLA Ops:
  0.6 0.0 copy-start.2
  0.7 12.7 %copy.47 = bf16[256,2,8192]{2,0,1:T(8,128)(2,1)} copy(bf16[256,2,8192]{2,1,0:T(2,128)(2,1)} %param.13) | data formatting | bytes 16777216 | tf_op args[0]
  13.3 0.0 copy-done.2
  13.3 0.0 copy-start.6
  13.3 4.6 %copy.48 = bf16[128,2,8192]{2,0,1:T(8,128)(2,1)} copy(bf16[128,2,8192]{2,1,0:T(2,128)(2,1)S(1)} %copy-done.2) | data formatting | bytes 8388608 | tf_op args[1]
  17.9 0.0 copy-done.6
  17.9 1.0 compare_convert_fusion.pick_ref
  19.0 0.0 copy-start.4
  19.0 0.0 copy-start.5
  19.0 34.5 %scores.1 = (f32[1024,128]{1,0:T(8,128)}, bf16[2,1024,8192]{2,1,0:T(8,128)(2,1)}) custom-call(bf16[1024,192]{1,0:T(8,128)(2,1)} %compare_convert_fusion.pick_ref, bf16[192,8192]{1,0:T(8,128)(2,1)} %constant.47.clone.cos_ref, bf16[192,8192]{1,0:T(8,128)(2,1)} %constant.48.clone.sin_ref, bf16[2,256,8192]{2,1,0:T(8,128)(2,1)} %bitcast.57, ...), custom_call_target="tpu_custom_call" | custom-call | tf_op jit(solution)/shard_map/scores/pallas_call | solution.py:432
  53.5 0.0 copy-start.1
  53.5 1.3 reduce_max.21
  54.8 1.4 exponential_reduce_fusion
  56.3 14.4 %all-gather.1 = f32[8,2,256]{2,1,0:T(2,128)S(1)} all-gather(f32[1,2,256]{2,1,0:T(2,128)S(1)} %maximum_bitcast_fusion), channel_id=2, replica_groups=mesh['img'=4,'ori'=8] {'ori'}, dimensions={0}, use_global_device_ids=true | all-gather | bytes 18432 | tf_op jit(solution)/shard_map/all_gather | solution.py:458
  70.7 0.0 copy-done.4
  70.7 0.2 convolution_bitcast_fusion
  70.9 0.1 slice.13
  71.0 0.2 copy.35
  71.2 0.2 copy.36
  71.4 0.3 subtract_reduce_fusion
  71.6 0.1 select_reduce_fusion
  71.8 0.0 copy-start.3
  71.8 8.2 %scatter_custom_fusion = s32[6144]{0:T(1024)S(1)} fusion(s32[2048]{0:T(1024)S(1)} %bitcast.74, s32[2048]{0:T(1024)} %bitcast.77, s32[]{:T(128)} %constant.42.clone.1), kind=kCustom, calls=%fused_computation.18 | custom fusion | bytes 25088 | tf_op jit(solution)/shard_map/scatter | solution.py:415
  80.1 0.1 reshape.143
  80.2 0.0 copy-done.5
  80.2 1.3 broadcast_in_dim.32.id_ref
  81.5 0.6 all_to_all.9
  82.1 4.6 %all-to-all-start = ((s32[32,1,192]{2,1,0:T(1,128)}), s32[32,1,192]{2,1,0:T(1,128)S(1)}, u32[]{:S(2)}, u32[]{:S(2)}) async-start(s32[32,1,192]{2,1,0:T(1,128)} %all_to_all.9), calls=%async_computation | async-start | bytes 65536 | tf_op jit(solution)/shard_map/all_to_all | solution.py:462
  86.8 0.0 copy-done.1
  86.8 0.2 copy.38
  87.1 0.8 fusion.prob_ref
  87.9 57.6 %slices.1.term_ref = bf16[2048,256]{1,0:T(8,128)(2,1)} custom-call(bf16[2,1024,8192]{2,1,0:T(8,128)(2,1)} %get-tuple-element.11.aligned_ref, bf16[128,1024]{1,0:T(8,128)(2,1)} %fusion.prob_ref, bf16[16,2,128,128]{3,2,1,0:T(8,128)(2,1)} %broadcast_in_dim.32.id_ref, bf16[8192,128]{1,0:T(8,128)(2,1)} %bitcast.63), custom_call_target="tpu_custom_call" | custom-call | tf_op jit(solution)/shard_map/slices/pallas_call | solution.py:474
  145.5 0.0 copy-done.3
  145.5 10.6 %place.1 = bf16[6144,256]{1,0:T(8,128)(2,1)} custom-call(s32[1,2048]{1,0:T(1,128)} %bitcast.65, bf16[2048,256]{1,0:T(8,128)(2,1)} %slices.1.term_ref), custom_call_target="tpu_custom_call" | custom-call | tf_op jit(solution)/shard_map/place/pallas_call | solution.py:498
  156.1 0.0 all-to-all-done
  156.1 7.5 %all-to-all-start.1 = ((bf16[32,192,256]{2,1,0:T(8,128)(2,1)}), bf16[32,192,256]{2,1,0:T(8,128)(2,1)S(1)}, u32[]{:S(2)}, u32[]{:S(2)}) async-start(bf16[32,192,256]{2,1,0:T(8,128)(2,1)} %bitcast.59), calls=%async_computation.1 | async-start | bytes 6291456 | tf_op jit(solution)/shard_map/all_to_all | solution.py:507
  163.6 0.6 log_add_fusion
  164.1 0.1 reduce.7
  164.2 0.7 reshape.144.cell_ref
  164.9 71.3 %all-to-all-done.1 = bf16[32,192,256]{2,1,0:T(8,128)(2,1)S(1)} async-done(((bf16[32,192,256]{2,1,0:T(8,128)(2,1)}), bf16[32,192,256]{2,1,0:T(8,128)(2,1)S(1)}, u32[]{:S(2)}, u32[]{:S(2)}) %all-to-all-start.1) | async-done | bytes 3145760 | tf_op jit(solution)/shard_map/all_to_all | solution.py:507
  236.2 0.0 copy-start
  236.2 1.7 copy-done
  237.8 58.8 %transform.1 = bf16[8,32,32,128]{3,2,1,0:T(8,128)(2,1)} custom-call(s32[1,6144]{1,0:T(1,128)} %reshape.144.cell_ref, bf16[6144,256]{1,0:T(8,128)(2,1)} %bitcast.60, bf16[2,2,256,512]{3,2,1,0:T(8,128)(2,1)} %constant.49.clone.z_ref, bf16[4,256,256]{2,1,0:T(8,128)(2,1)} %constant.50.clone.dft_ref, bf16[128,128]{1,0:T(8,128)(2,1)} %constant.51.clone.turn_ref), custom_call_target="tpu_custom_call" | custom-call | tf_op jit(solution)/shard_map/transform/pallas_call | solution.py:523
  296.6 8.7 %along_x.1 = f32[128,32,256]{2,1,0:T(8,128)} custom-call(bf16[4,256,256]{2,1,0:T(8,128)(2,1)} %constant.50.clone.dft_ref, bf16[256,32,128]{2,1,0:T(8,128)(2,1)} %bitcast.61), custom_call_target="tpu_custom_call" | custom-call | tf_op jit(solution)/shard_map/along_x/pallas_call | solution.py:543
  (21 shorter events, 0.2 us)
Async XLA Ops:
  0.6 12.7 %copy-start.2 = (bf16[128,2,8192]{2,1,0:T(2,128)(2,1)S(1)}, bf16[128,2,8192]{2,1,0:T(2,128)(2,1)}, u32[]{:S(2)}) copy-start(bf16[128,2,8192]{2,1,0:T(2,128)(2,1)} %param.14) | copy-start | bytes 12582916
  13.3 4.6 %copy-start.6 = (s32[256,4]{0,1:T(4,128)S(1)}, s32[256,4]{0,1:T(4,128)}, u32[]{:S(2)}) copy-start(s32[256,4]{0,1:T(4,128)} %param.16) | copy-start | bytes 12292
  19.0 51.7 %copy-start.4 = (s32[128,16]{0,1:T(8,128)S(1)}, s32[128,16]{0,1:T(8,128)}, u32[]{:S(2)}) copy-start(s32[128,16]{0,1:T(8,128)} %param.17) | copy-start | bytes 24580
  19.0 61.2 %copy-start.5 = (s32[128,16]{0,1:T(8,128)S(1)}, s32[128,16]{0,1:T(8,128)}, u32[]{:S(2)}) copy-start(s32[128,16]{0,1:T(8,128)} %param.19) | copy-start | bytes 24580
  53.5 33.3 %copy-start.1 = (f32[1024,128]{1,0:T(8,128)S(1)}, f32[1024,128]{1,0:T(8,128)}, u32[]{:S(2)}) copy-start(f32[1024,128]{1,0:T(8,128)} %get-tuple-element.8) | copy-start | bytes 1572868
  71.8 73.6 %copy-start.3 = (s32[16,128]{1,0:T(8,128)}, s32[16,128]{1,0:T(8,128)S(1)}, u32[]{:S(2)}) copy-start(s32[16,128]{1,0:T(8,128)S(1)} %add_add_fusion) | copy-start | bytes 24580
  82.1 74.0 %all-to-all-start = ((s32[32,1,192]{2,1,0:T(1,128)}), s32[32,1,192]{2,1,0:T(1,128)S(1)}, u32[]{:S(2)}, u32[]{:S(2)}) async-start(s32[32,1,192]{2,1,0:T(1,128)} %all_to_all.9), calls=%async_computation | async-start | bytes 65536 | tf_op jit(solution)/shard_map/all_to_all | solution.py:462
  156.1 80.1 %all-to-all-start.1 = ((bf16[32,192,256]{2,1,0:T(8,128)(2,1)}), bf16[32,192,256]{2,1,0:T(8,128)(2,1)S(1)}, u32[]{:S(2)}, u32[]{:S(2)}) async-start(bf16[32,192,256]{2,1,0:T(8,128)(2,1)} %bitcast.59), calls=%async_computation.1 | async-start | bytes 6291456 | tf_op jit(solution)/shard_map/all_to_all | solution.py:507
  236.2 1.7 copy-start
